TPU v7x, 32 devices: a whole 2x2x4 slice. The times are simulated.
32 devices in a mesh: groups: 2 (over y), sec: 4 (over z), row: 2 (over x), rep: 2 (over core).
Axes of the slice: x: 2, y: 2, z: 4, core: 2. Of those that a mesh axis runs over, the one named last changes fastest.
Arguments:
- psi: bfloat16 [128, 256, 256], P(('groups', 'sec')), parts along dimension 0, may hold values from -6 to 6
- left_environment_blocks: bfloat16 [16, 24, 256, 256], P(('groups', 'sec'), 'rep', 'row'), parts along dimension 0, may hold values from -0.078125 to 0.078125
- right_env: bfloat16 [16, 24, 256, 256], P(('groups', 'sec'), 'rep', 'row'), parts along dimension 0, may hold values from -0.375 to 0.375
- pair_dest: int32 [128, 1], P(('groups', 'sec')), parts along dimension 0, may hold values from 0 to 3; in each aligned block of 16 rows (0 to 15, 16 to 31, ...) at most 8 rows name the same one
- pair_left_sector: int32 [128], P(('groups', 'sec')), parts along dimension 0, may hold values from 0 to 1
- pair_right: int32 [128], P(('groups', 'sec')), parts along dimension 0, may hold values from 0 to 1
Outputs:
- mixed: bfloat16 [8, 32, 256, 256], P(('groups', 'sec'), 'rep', 'row'), parts along dimension 0
There are 2 independent parts, one for each index of `groups`. A program takes and returns all parts, laid end to end along the dimension named above; each array names one. Nothing has to cross between parts.
Inputs may be any that keep to these rules, and one draw needn't show every extreme that they name: `pair_dest`: among the 16 pairs of one sec index no destination is named more than 8 times, a bound that some block reaches.
All inputs are finite; a program needn't handle non-finite values.
Results may differ from a plain program's by a relative error of at most 0.005.
Values may be sent and summed in bfloat16 or wider, within the bound.
A program may use at most 192 MiB of HBM per device.

v0:
```python
import jax
import jax.numpy as jnp
from jax import lax
from jax.sharding import PartitionSpec as P


def slot_terms(blocks, owners, weights, capacity):
    group_count = blocks.shape[0] // capacity

    def per_group(group):
        span_rows = lax.dynamic_slice_in_dim(blocks, group * capacity, capacity, 0)
        span_owners = lax.dynamic_slice_in_dim(owners, group * capacity, capacity, 0)
        current_weights = weights[jnp.maximum(span_owners, 0)]
        return jnp.einsum(
            "cwab,cwbd->cad", span_rows, current_weights, preferred_element_type=jnp.float32
        )

    stacked = lax.map(per_group, jnp.arange(group_count))
    return stacked.reshape((blocks.shape[0], blocks.shape[2], weights.shape[3]))


def body(psi, left_environment_blocks, right_env, pair_dest, pair_left_sector, pair_right):
    sector_count = lax.axis_size("sec")
    this_index = lax.axis_index("sec")
    pair_count = psi.shape[0]
    capacity = 2 * pair_count // sector_count
    slot_count = capacity * sector_count
    targets = pair_dest[:, 0]
    all_dest, all_right = (
        lax.all_gather(targets, "sec", axis=0, tiled=True),
        lax.all_gather(pair_right, "sec", axis=0, tiled=True),
    )
    chosen = left_environment_blocks[pair_left_sector]
    product = jnp.einsum("pwab,pbc->pwac", chosen, psi, preferred_element_type=jnp.float32).astype(
        jnp.bfloat16
    )
    onehot = (targets[:, None] == jnp.arange(sector_count)[None, :]).astype(jnp.int32)
    ranking = jnp.sum(onehot * (jnp.cumsum(onehot, axis=0) - onehot), axis=1)
    slot_index = targets * capacity + ranking
    outgoing = (
        jnp.zeros((slot_count,) + product.shape[1:], jnp.bfloat16).at[slot_index].set(product)
    )
    grid_dest = all_dest.reshape(sector_count, pair_count)
    grid_right = all_right.reshape(sector_count, pair_count)
    grid_hot = (grid_dest[:, :, None] == jnp.arange(sector_count)[None, None, :]).astype(jnp.int32)
    grid_rank = jnp.sum(grid_hot * (jnp.cumsum(grid_hot, axis=1) - grid_hot), axis=-1)
    matches = (
        (grid_dest == this_index)[:, :, None]
        & (grid_rank[:, :, None] == jnp.arange(capacity)[None, None, :])
    ).astype(jnp.int32)
    slot_sector = (jnp.sum(matches * (grid_right + 1)[:, :, None], axis=1) - 1).reshape(slot_count)
    right_rows = lax.all_gather(right_env, "row", axis=2, tiled=True)
    arrived = lax.all_to_all(outgoing, "sec", split_axis=0, concat_axis=0, tiled=True)
    summed = lax.psum_scatter(
        slot_terms(arrived, slot_sector, right_rows, capacity),
        "rep",
        scatter_dimension=0,
        tiled=True,
    )
    return summed.astype(jnp.bfloat16)[None]


def solution(mesh):
    placed = (
        P(("groups", "sec"), None, None),
        P(("groups", "sec"), "rep", "row", None),
        P(("groups", "sec"), "rep", "row", None),
        P(("groups", "sec"), None),
        P(("groups", "sec")),
        P(("groups", "sec")),
    )
    return jax.shard_map(
        body,
        mesh=mesh,
        in_specs=placed,
        out_specs=P(("groups", "sec"), "rep", "row", None),
        check_vma=False,
    )
```

profile of v0, /device:TPU:1, one launch (start us, length us, event | category | flops | bytes accessed | tf_op | source)
XLA Modules:
  0.0 721.1 jit_solution(15906038615009558703)
XLA Ops:
  6.5 0.0 copy-start
  6.5 0.9 fusion.12
  7.4 0.8 select_reduce_fusion.2
  8.3 0.7 fusion.13
  9.0 0.7 compare_select_fusion
  9.6 7.5 %gather_fusion.1 = bf16[16,12,128,256]{3,2,1,0:T(8,128)(2,1)} fusion(bf16[2,12,128,256]{3,2,1,0:T(8,128)(2,1)} %param.9, s32[1024]{0:T(1024)S(1)} %pad_clamp_fusion.1), kind=kCustom, calls=%fused_computation.1 | custom fusion | bytes 25165888 | tf_op jit(solution)/shard_map/gather | solution.py:33
  17.1 0.0 copy-done
  17.1 9.2 %convolution_convert_fusion = bf16[16,12,128,256]{3,2,1,0:T(8,128)(2,1)} fusion(bf16[16,12,128,256]{3,2,1,0:T(8,128)(2,1)} %gather_fusion.1, bf16[16,256,256]{2,1,0:T(8,128)(2,1)S(1)} %copy-done), kind=kOutput, calls=%fused_computation.10 | convolution fusion | flops 3227516928 | bytes 27262976 | tf_op jit(solution)/shard_map/pwab,pbc->pwac/dot_general | solution.py:34
  26.2 8.4 %broadcast_in_dim.27 = bf16[32,12,128,256]{3,2,1,0:T(8,128)(2,1)} broadcast(bf16[]{:T(256)} %constant.40.clone.1), dimensions={} | broadcast | bytes 25165826 | tf_op jit(solution)/shard_map/broadcast_in_dim | solution.py:41
  34.7 37.5 %scatter_fusion = bf16[32,12,128,256]{3,2,1,0:T(8,128)(2,1)} fusion(bf16[32,12,128,256]{3,2,1,0:T(8,128)(2,1)} %broadcast_in_dim.27, s32[16]{0:T(128)S(1)} %fusion.13, bf16[16,12,128,256]{3,2,1,0:T(8,128)(2,1)} %convolution_convert_fusion), kind=kCustom, calls=%fused_computation.2 | custom fusion | bytes 37748800 | tf_op jit(solution)/shard_map/scatter | solution.py:41
  72.2 8.6 %all-to-all-start = ((bf16[32,12,128,256]{3,2,1,0:T(8,128)(2,1)}), bf16[32,12,128,256]{3,2,1,0:T(8,128)(2,1)}, u32[]{:S(2)}, u32[]{:S(2)}) async-start(bf16[32,12,128,256]{3,2,1,0:T(8,128)(2,1)} %scatter_fusion), calls=%async_computation | async-start | bytes 50331648 | tf_op jit(solution)/shard_map/all_to_all | solution.py:53
  80.8 0.0 all-gather.3.cloned.1.call-start
  80.8 0.7 all-gather.3.cloned.1.call-update
  81.5 0.0 reduce-scatter.2.cloned.1.call-start
  81.6 0.0 copy-done.4
  81.6 0.6 dynamic-slice
  82.9 0.0 copy-done.3
  82.9 0.2 dynamic-update-slice.1
  83.1 0.0 copy-done.2
  83.1 0.1 bitcast_dynamic-update-slice_fusion
  83.2 541.1 %all-reduce.2 = (s32[64]{0:T(128)S(1)}, s32[64]{0:T(128)S(1)}) all-reduce(s32[64]{0:T(128)S(1)} %dynamic-update-slice.1, s32[64]{0:T(128)S(1)} %bitcast_dynamic-update-slice_fusion), channel_id=1, replica_groups=mesh['groups'=2,'sec'=4,'row'=2,'rep'=2] {'sec'}, use_global_device_ids=true, to_apply=%add.1 | all-reduce | flops 128 | bytes 1024
  624.3 0.1 reshape.28
  624.4 0.1 add.42
  624.5 0.1 fusion.10
  624.6 0.2 select_reduce_fusion
  624.8 0.1 select_reduce_fusion.1
  625.0 0.1 sub.15
  625.1 0.0 all-to-all-done
  625.1 74.3 %while.10 = (s32[]{:T(128)}, f32[4,8,128,256]{3,2,1,0:T(8,128)}, s32[4]{0:T(128)S(1)}, bf16[32,12,128,256]{3,2,1,0:T(8,128)(2,1)}, s32[32]{0:T(128)S(1)}, /*inde...) while((s32[]{:T(128)}, f32[4,8,128,256]{3,2,1,0:T(8,128)}, ...), condition=%wide.region_7.8_spmd, body=%wide.region_6.7_spmd.sunk | while | flops 1610613760 | bytes 45093672 | solution.py:18
  625.1 0.6 dynamic_slice.22
  626.3 0.1 dynamic-slice_maximum_fusion.2
  626.4 7.9 %gather_fusion = bf16[8,12,256,256]{3,2,1,0:T(8,128)(2,1)} fusion(bf16[2,12,256,256]{3,2,1,0:T(8,128)(2,1)} %get-tuple-element.114, s32[1024]{0:T(1024)S(1)} %pad_clamp_fusion.3), kind=kCustom, calls=%fused_computation.clone.1 | custom fusion | bytes 25165856 | tf_op jit(solution)/shard_map/while/body/eval_jaxpr/gather | solution.py:13
  634.3 9.2 %fusion.21 = f32[4,8,128,256]{3,2,1,0:T(8,128)} fusion(f32[4,8,128,256]{3,2,1,0:T(8,128)} %get-tuple-element.100, s32[]{:T(128)} %get-tuple-element.99, bf16[8,12,256,256]{3,2,1,0:T(8,128)(2,1)} %gather_fusion, bf16[32,12,128,256]{3,2,1,0:T(8,128)(2,1)} %get-tuple-element.112, s32[]{:T(128)S(6)} %select_n.19), kind=kOutput, calls=%fused_computation.6.clone.1 | convolution fusion | flops 1610612736 | bytes 19923460 | tf_op jit(solution)/shard_map/while/body/eval_jaxpr/cwab,cwbd->cad/dot_general | solution.py:14
  643.5 0.6 dynamic_slice.22
  644.7 0.1 dynamic-slice_maximum_fusion.2
  644.8 8.1 %gather_fusion = bf16[8,12,256,256]{3,2,1,0:T(8,128)(2,1)} fusion(bf16[2,12,256,256]{3,2,1,0:T(8,128)(2,1)} %get-tuple-element.114, s32[1024]{0:T(1024)S(1)} %pad_clamp_fusion.3), kind=kCustom, calls=%fused_computation.clone.1 | custom fusion | bytes 25165856 | tf_op jit(solution)/shard_map/while/body/eval_jaxpr/gather | solution.py:13
  652.9 9.2 %fusion.21 = f32[4,8,128,256]{3,2,1,0:T(8,128)} fusion(f32[4,8,128,256]{3,2,1,0:T(8,128)} %get-tuple-element.100, s32[]{:T(128)} %get-tuple-element.99, bf16[8,12,256,256]{3,2,1,0:T(8,128)(2,1)} %gather_fusion, bf16[32,12,128,256]{3,2,1,0:T(8,128)(2,1)} %get-tuple-element.112, s32[]{:T(128)S(6)} %select_n.19), kind=kOutput, calls=%fused_computation.6.clone.1 | convolution fusion | flops 1610612736 | bytes 19923460 | tf_op jit(solution)/shard_map/while/body/eval_jaxpr/cwab,cwbd->cad/dot_general | solution.py:14
  662.1 0.6 dynamic_slice.22
  663.3 0.1 dynamic-slice_maximum_fusion.2
  663.4 8.1 %gather_fusion = bf16[8,12,256,256]{3,2,1,0:T(8,128)(2,1)} fusion(bf16[2,12,256,256]{3,2,1,0:T(8,128)(2,1)} %get-tuple-element.114, s32[1024]{0:T(1024)S(1)} %pad_clamp_fusion.3), kind=kCustom, calls=%fused_computation.clone.1 | custom fusion | bytes 25165856 | tf_op jit(solution)/shard_map/while/body/eval_jaxpr/gather | solution.py:13
  671.6 9.2 %fusion.21 = f32[4,8,128,256]{3,2,1,0:T(8,128)} fusion(f32[4,8,128,256]{3,2,1,0:T(8,128)} %get-tuple-element.100, s32[]{:T(128)} %get-tuple-element.99, bf16[8,12,256,256]{3,2,1,0:T(8,128)(2,1)} %gather_fusion, bf16[32,12,128,256]{3,2,1,0:T(8,128)(2,1)} %get-tuple-element.112, s32[]{:T(128)S(6)} %select_n.19), kind=kOutput, calls=%fused_computation.6.clone.1 | convolution fusion | flops 1610612736 | bytes 19923460 | tf_op jit(solution)/shard_map/while/body/eval_jaxpr/cwab,cwbd->cad/dot_general | solution.py:14
  680.7 0.6 dynamic_slice.22
  682.0 0.1 dynamic-slice_maximum_fusion.2
  682.0 8.1 %gather_fusion = bf16[8,12,256,256]{3,2,1,0:T(8,128)(2,1)} fusion(bf16[2,12,256,256]{3,2,1,0:T(8,128)(2,1)} %get-tuple-element.114, s32[1024]{0:T(1024)S(1)} %pad_clamp_fusion.3), kind=kCustom, calls=%fused_computation.clone.1 | custom fusion | bytes 25165856 | tf_op jit(solution)/shard_map/while/body/eval_jaxpr/gather | solution.py:13
  690.2 9.2 %fusion.21 = f32[4,8,128,256]{3,2,1,0:T(8,128)} fusion(f32[4,8,128,256]{3,2,1,0:T(8,128)} %get-tuple-element.100, s32[]{:T(128)} %get-tuple-element.99, bf16[8,12,256,256]{3,2,1,0:T(8,128)(2,1)} %gather_fusion, bf16[32,12,128,256]{3,2,1,0:T(8,128)(2,1)} %get-tuple-element.112, s32[]{:T(128)S(6)} %select_n.19), kind=kOutput, calls=%fused_computation.6.clone.1 | convolution fusion | flops 1610612736 | bytes 19923460 | tf_op jit(solution)/shard_map/while/body/eval_jaxpr/cwab,cwbd->cad/dot_general | solution.py:14
  699.4 0.0 reduce-scatter.2.cloned.1.call-update
  699.4 12.1 %reduce-scatter.2.cloned.1.call-done = f32[16,128,256]{2,1,0:T(8,128)} async-done(((f32[32,128,256]{2,1,0:T(8,128)}), f32[16,128,256]{2,1,0:T(8,128)}) %reduce-scatter.2.cloned.1.call-update) | async-done | bytes 2097168 | tf_op jit(solution)/shard_map/reduce_scatter | solution.py:54
  711.5 2.7 convert_bitcast_fusion
  (20 shorter events, 0.2 us)
Async XLA Ops:
  6.5 10.5 %copy-start = (bf16[16,256,256]{2,1,0:T(8,128)(2,1)S(1)}, bf16[16,256,256]{2,1,0:T(8,128)(2,1)}, u32[]{:S(2)}) copy-start(bf16[16,256,256]{2,1,0:T(8,128)(2,1)} %param.8) | copy-start | bytes 6291460
  72.2 9.4 %copy-start.4 = (u32[32]{0:T(128)S(1)}, u32[32]{0:T(128)}, u32[]{:S(2)}) copy-start(u32[32]{0:T(128)} %constant.52) | copy-start | bytes 388
  72.2 10.6 %copy-start.3 = (s32[16]{0:T(128)S(1)}, s32[16]{0:T(128)}, u32[]{:S(2)}) copy-start(s32[16]{0:T(128)} %param.13) | copy-start | bytes 196
  72.2 10.9 %copy-start.2 = (s32[16,1]{0,1:T(1,128)S(1)}, s32[16,1]{0,1:T(1,128)}, u32[]{:S(2)}) copy-start(s32[16,1]{0,1:T(1,128)} %param.11) | copy-start | bytes 196
  72.2 552.8 %all-to-all-start = ((bf16[32,12,128,256]{3,2,1,0:T(8,128)(2,1)}), bf16[32,12,128,256]{3,2,1,0:T(8,128)(2,1)}, u32[]{:S(2)}, u32[]{:S(2)}) async-start(bf16[32,12,128,256]{3,2,1,0:T(8,128)(2,1)} %scatter_fusion), calls=%async_computation | async-start | bytes 50331648 | tf_op jit(solution)/shard_map/all_to_all | solution.py:53
  80.8 544.2 %all-gather.3.cloned.1.call-start = ((), (), s32[]{:S(2)}) async-start(), calls=%async_computation.2 | async-start | bytes 4718592 | tf_op jit(solution)/shard_map/all_gather | solution.py:52
  81.5 630.0 %reduce-scatter.2.cloned.1.call-start = ((), (), s32[]{:S(2)}) async-start(), calls=%async_computation.3 | async-start | bytes 6291456 | tf_op jit(solution)/shard_map/reduce_scatter | solution.py:54
  699.4 14.8 %copy-start.1 = (bf16[16,256,256]{2,1,0:T(8,128)(2,1)S(1)}, bf16[16,256,256]{2,1,0:T(8,128)(2,1)}, u32[]{:S(2)}) copy-start(bf16[16,256,256]{2,1,0:T(8,128)(2,1)} %param.8) | copy-start | bytes 6291460
Sparse Core Ops, SparseCore 0:
  83.2 47.2 all-gather.2
  699.5 11.9 reduce-scatter.1
where the time goes:
time: 722 us; the launch traced here: 721 us
  blocking collectives  541 us (75%)
  local copies, waits for them, and re-layouts  89.3 us (12%)
  matrix products  45.9 us (6%)
  between operations  14.1 us (2%)
  waiting for transfers between devices  12.8 us (2%)
  starting transfers between devices  8.64 us (1%)
    unnamed x1, blocking collectives  541 us
    scatter x1, local copies, waits for them, and re-layouts, body(): jnp.zeros((slot_count,) + product.shape[1:], jnp.bfloat16).at[slot_index]  37.5 us
    dot_general x4, matrix products, per_group(): jnp.einsum('cwab,cwbd->cad', span_rows, current_weights, preferred_elemen...  36.7 us
    gather x4, local copies, waits for them, and re-layouts, per_group(): current_weights = weights[jnp.maximum(span_owners, 0)]  32.3 us
  transfers between devices with their start and end apart: 3, of which 1 were waited for; matrix products, arithmetic and copies ran while one was open for 0% of the time, Pallas kernels for 0%

commit v1 on v0

v1 whole, which is shorter than its diff:
```python
import functools

import jax
import jax.numpy as jnp
from jax import lax
from jax.experimental import pallas as pl
from jax.experimental.pallas import tpu as pltpu
from jax.sharding import PartitionSpec as P

MESH = pl.DeviceIdType.MESH


def remote(src, dst, send, recv, where):
    return pltpu.make_async_remote_copy(
        src_ref=src, dst_ref=dst, send_sem=send, recv_sem=recv, device_id=where, device_id_type=MESH
    )


def kernel(
    sizes,
    fill_ref,
    left_ref,
    right_ref,
    psi_ref,
    lenv_ref,
    renv_ref,
    out_ref,
    stage,
    psi_in,
    lfar,
    rfull,
    acc,
    peer,
    psi_send,
    psi_recv,
    row_send,
    row_recv,
    rep_send,
    rep_recv,
    rrow_send,
    rrow_recv,
    up_send,
    down_send,
    l_recv,
    sum_send,
    sum_recv,
):
    secs, rows, capacity, chunks = sizes
    bonds, height, width = lenv_ref.shape[1:]
    step = bonds // chunks
    part = width // (2 * rows)
    half = secs // 2
    me = lax.axis_index("sec")
    row = lax.axis_index("row")
    rep = lax.axis_index("rep")
    other = 1 - rep
    mine = row * 2 + rep

    def bars(q):
        return pl.ds(pl.multiple_of(q * part, part), part)

    barrier = pltpu.get_barrier_semaphore()
    for h in range(1, secs):
        pl.semaphore_signal(
            barrier, inc=1, device_id={"sec": lax.rem(me + h, secs)}, device_id_type=MESH
        )
    for h in range(1, rows):
        pl.semaphore_signal(
            barrier, inc=1, device_id={"row": lax.rem(row + h, rows)}, device_id_type=MESH
        )
    pl.semaphore_signal(barrier, inc=1, device_id={"rep": other}, device_id_type=MESH)
    pl.semaphore_wait(barrier, secs + rows - 1)

    def l_copy(source, c, src, direction):
        sends = up_send if direction == 1 else down_send
        return remote(
            src,
            lfar.at[source, c],
            sends.at[source, c],
            l_recv.at[source, c],
            {"sec": me + direction},
        )

    def chunk_of(c):
        return lenv_ref.at[:, pl.ds(c * step, step)]

    def fill(d):
        for j in range(capacity):
            p = fill_ref[d * capacity + j]
            block = psi_ref[jnp.maximum(p, 0), bars(mine), :]
            stage[d, j] = jnp.where(p >= 0, block, jnp.zeros_like(block))

    def psi_copy(d, source):
        return remote(
            stage.at[d],
            psi_in.at[source, mine],
            psi_send.at[d],
            psi_recv.at[source],
            {"sec": d},
        )

    for h in range(1, secs):
        d = lax.rem(me + h, secs)
        fill(d)
        psi_copy(d, me).start()

    for c in range(chunks):

        @pl.when(me + 1 < secs)
        def _():
            l_copy(me, c, chunk_of(c), 1).start()

        @pl.when(me > 0)
        def _():
            l_copy(me, c, chunk_of(c), -1).start()

    def r_copy(h, owner):
        return remote(
            renv_ref,
            rfull.at[owner],
            rrow_send.at[h],
            rrow_recv.at[owner],
            {"row": lax.rem(row + h, rows)},
        )

    for h in range(1, rows):
        r_copy(h, row).start()
    rfull[row] = renv_ref[...]

    for j in range(capacity):
        p = fill_ref[me * capacity + j]
        for q in range(2 * rows):
            block = psi_ref[jnp.maximum(p, 0), pl.ds(q * part, part), :]
            psi_in[me, q, j] = jnp.where(p >= 0, block, jnp.zeros_like(block))

    def row_copy(source, h, to):
        return remote(
            psi_in.at[source, mine],
            psi_in.at[source, mine],
            row_send.at[source, h],
            row_recv.at[source, row],
            {"row": to},
        )

    def rep_copy(source, r):
        bar = r * 2 + rep
        return remote(
            psi_in.at[source, bar],
            psi_in.at[source, bar],
            rep_send.at[source, r],
            rep_recv.at[source, r],
            {"rep": other},
        )

    for h in range(1, secs):
        source = lax.rem(me + secs - h, secs)
        psi_copy(source, source).wait_recv()
        for k in range(1, rows):
            row_copy(source, k, lax.rem(row + k, rows)).start()
        rep_copy(source, row).start()

    for h in range(1, rows):
        owner = lax.rem(row + h, rows)
        r_copy(h, owner).wait_recv()

    for h in range(1, secs):
        source = lax.rem(me + secs - h, secs)
        for k in range(1, rows):
            owner = lax.rem(row + k, rows)
            bar = owner * 2 + rep
            remote(
                psi_in.at[source, bar],
                psi_in.at[source, bar],
                row_send.at[source, k],
                row_recv.at[source, owner],
                {"row": owner},
            ).wait_recv()
            rep_copy(source, owner).start()

    for h in range(1, secs):
        source = lax.rem(me + secs - h, secs)
        for r in range(rows):
            rep_copy(source, r).wait_recv()

    def work(source, c, block):
        def one(j, carry):
            at = source * capacity + j
            ls = left_ref[at]
            rs = right_ref[at]
            low, high = block(0), block(1)
            a = jnp.where(ls == 0, low, high).reshape(step * height, width)
            x = psi_in[source, :, j].reshape(width, width)
            product = jnp.dot(a, x, preferred_element_type=jnp.float32).astype(jnp.bfloat16)
            total = None
            for w in range(step):
                b = rfull[:, rs, c * step + w].reshape(width, width)
                term = jnp.dot(
                    product[w * height : (w + 1) * height], b, preferred_element_type=jnp.float32
                )
                total = term if total is None else total + term
            if c == 0:
                acc[source, j] = total
            else:
                acc[source, j] += total
            return carry

        lax.fori_loop(0, capacity, one, 0)

    def sum_copy(source):
        return remote(
            acc.at[source],
            peer.at[lax.rem(source, half)],
            sum_send.at[source],
            sum_recv.at[lax.rem(source, half)],
            {"rep": other},
        )

    def hand_over(source):
        @pl.when(source // half != rep)
        def _():
            sum_copy(source).start()

    for c in range(chunks):
        work(me, c, lambda s: lenv_ref[s, pl.ds(c * step, step)])
    hand_over(me)

    for h in range(1, secs):
        for c in range(chunks):

            @pl.when(me >= h)
            def _():
                source = me - h
                l_copy(source, c, lfar.at[source, c], 1).wait_recv()

                @pl.when(me + 1 < secs)
                def _():
                    l_copy(source, c, lfar.at[source, c], 1).start()

            @pl.when(me + h < secs)
            def _():
                source = me + h
                l_copy(source, c, lfar.at[source, c], -1).wait_recv()

                @pl.when(me > 0)
                def _():
                    l_copy(source, c, lfar.at[source, c], -1).start()

            @pl.when(me >= h)
            def _():
                source = me - h
                work(source, c, lambda s: lfar[source, c, s])
                if c == chunks - 1:
                    hand_over(source)

            @pl.when(me + h < secs)
            def _():
                source = me + h
                work(source, c, lambda s: lfar[source, c, s])
                if c == chunks - 1:
                    hand_over(source)

    def finish(i, carry):
        source = rep * half + i
        sum_copy(source).wait_recv()

        def one(j, carry):
            out_ref[i * capacity + j] = (acc[source, j] + peer[i, j]).astype(out_ref.dtype)
            return carry

        return lax.fori_loop(0, capacity, one, carry)

    lax.fori_loop(0, half, finish, 0)

    for h in range(1, secs):
        d = lax.rem(me + h, secs)
        psi_copy(d, me).wait_send()
        for k in range(1, rows):
            row_copy(d, k, lax.rem(row + k, rows)).wait_send()
        for r in range(rows):
            rep_copy(d, r).wait_send()
    for h in range(1, rows):
        r_copy(h, row).wait_send()
    for c in range(chunks):
        for h in range(secs):

            @pl.when((me >= h) & (me + 1 < secs))
            def _():
                l_copy(me - h, c, lfar.at[me - h, c], 1).wait_send()

            @pl.when((me + h < secs) & (me > 0))
            def _():
                l_copy(me + h, c, lfar.at[me + h, c], -1).wait_send()

    def left(i, carry):
        sum_copy(other * half + i).wait_send()
        return carry

    lax.fori_loop(0, half, left, 0)


def body(rows, psi, left_environment_blocks, right_env, pair_dest, pair_left_sector, pair_right):
    secs = lax.axis_size("sec")
    me = lax.axis_index("sec")
    pairs = psi.shape[0]
    capacity = 2 * pairs // secs
    sectors, bonds, height, width = left_environment_blocks.shape
    chunks = 4
    step = bonds // chunks
    part = width // (2 * rows)
    code = pair_dest[:, 0] * 4 + pair_left_sector * 2 + pair_right
    codes = lax.all_gather(code, "sec", axis=0, tiled=True).reshape(secs, pairs)
    places = jnp.arange(pairs)
    slots = jnp.arange(capacity)

    def ranks(dest):
        same = dest[..., :, None] == dest[..., None, :]
        earlier = places[None, :] < places[:, None]
        return jnp.sum((same & earlier).astype(jnp.int32), axis=-1)

    targets = pair_dest[:, 0]
    match = (targets[None, None, :] == jnp.arange(secs)[:, None, None]) & (
        ranks(targets)[None, None, :] == slots[None, :, None]
    )
    fill = (jnp.sum(match.astype(jnp.int32) * (places + 1), axis=-1) - 1).reshape(-1)
    dest = codes // 4
    found = ((dest == me)[:, None, :] & (ranks(dest)[:, None, :] == slots[None, :, None])).astype(
        jnp.int32
    )
    at = jnp.sum(found * (codes % 4)[:, None, :], axis=-1).reshape(-1)
    bf16, f32 = jnp.bfloat16, jnp.float32
    dma = pltpu.SemaphoreType.DMA
    vmem = pl.BlockSpec(memory_space=pltpu.VMEM)
    smem = pl.BlockSpec(memory_space=pltpu.SMEM)
    out = pl.pallas_call(
        functools.partial(kernel, (secs, rows, capacity, chunks)),
        out_shape=jax.ShapeDtypeStruct((capacity * secs // 2, height, width), bf16),
        in_specs=[smem, smem, smem, vmem, vmem, vmem],
        out_specs=vmem,
        scratch_shapes=[
            pltpu.VMEM((secs, capacity, part, width), bf16),
            pltpu.VMEM((secs, 2 * rows, capacity, part, width), bf16),
            pltpu.VMEM((secs, chunks, sectors, step, height, width), bf16),
            pltpu.VMEM((rows, sectors, bonds, height, width), bf16),
            pltpu.VMEM((secs, capacity, height, width), f32),
            pltpu.VMEM((secs // 2, capacity, height, width), f32),
            dma((secs,)),
            dma((secs,)),
            dma((secs, rows)),
            dma((secs, rows)),
            dma((secs, rows)),
            dma((secs, rows)),
            dma((rows,)),
            dma((rows,)),
            dma((secs, chunks)),
            dma((secs, chunks)),
            dma((secs, chunks)),
            dma((secs // 2 * 2,)),
            dma((secs // 2,)),
        ],
        compiler_params=pltpu.CompilerParams(
            collective_id=0, has_side_effects=True, vmem_limit_bytes=56 * 1024 * 1024
        ),
        cost_estimate=pl.CostEstimate(
            flops=4 * secs * capacity * bonds * height * width * width,
            bytes_accessed=8 * 1024 * 1024,
            transcendentals=0,
        ),
    )(fill, at // 2, at % 2, psi, left_environment_blocks, right_env)
    return out[None]


def solution(mesh):
    placed = (
        P(("groups", "sec"), None, None),
        P(("groups", "sec"), "rep", "row", None),
        P(("groups", "sec"), "rep", "row", None),
        P(("groups", "sec"), None),
        P(("groups", "sec")),
        P(("groups", "sec")),
    )
    return jax.shard_map(
        functools.partial(body, mesh.shape["row"]),
        mesh=mesh,
        in_specs=placed,
        out_specs=P(("groups", "sec"), "rep", "row", None),
        check_vma=False,
    )
```

time: 722 us -> 166 us (0.23)
  blocking collectives: 541 us -> 7.25 us
  Pallas kernels: 0 us -> 150 us
  local copies, waits for them, and re-layouts: 89.3 us -> 4.29 us
  matrix products: 45.9 us -> 0 us
  between operations: 14.1 us -> 0.69 us
  waiting for transfers between devices: 12.8 us -> 0 us
  starting transfers between devices: 8.64 us -> 0 us
    unnamed x1, blocking collectives: 541 us -> 7.25 us
    pallas_call x0 -> x1, Pallas kernels: none -> 150 us  [body(): pl.pallas_call(functools.partial(kernel, (secs, rows, capacity, chunks)),...]
    dot_general x5 -> x0, matrix products: 45.9 us -> none  [the longest x4 36.7 us: per_group(): jnp.einsum('cwab,cwbd->cad', span_rows, current_weights, preferred_elemen...]
    gather x5 -> x0, local copies, waits for them, and re-layouts: 39.8 us -> none  [the longest x4 32.3 us: per_group(): current_weights = weights[jnp.maximum(span_owners, 0)]]
    scatter x1 -> x0, local copies, waits for them, and re-layouts: 37.5 us -> none  [body(): jnp.zeros((slot_count,) + product.shape[1:], jnp.bfloat16).at[slot_index]]
    reduce_scatter x1 -> x0, waiting for transfers between devices: 12.1 us -> none  [body(): lax.psum_scatter(slot_terms(arrived, slot_sector, right_rows, capacity),...]
    all_to_all x1 -> x0, starting transfers between devices: 8.56 us -> none  [body(): lax.all_to_all(outgoing, 'sec', split_axis=0, concat_axis=0, tiled=True)]
    broadcast_in_dim x1 -> x0, local copies, waits for them, and re-layouts: 8.45 us -> none  [body(): jnp.zeros((slot_count,) + product.shape[1:], jnp.bfloat16).at[slot_index]]
  transfers between devices with their start and end apart: 3 -> 0, of which waited for: 1 -> 0; matrix products, arithmetic and copies ran while one was open for 0% -> 0% of each run, Pallas kernels for 0% -> 0%
where the time goes in v1:
time: 166 us
  Pallas kernels  150 us (90%)
  blocking collectives  7.25 us (4%)
  local copies, waits for them, and re-layouts  4.29 us (3%)
  other arithmetic  3.53 us (2%)
    pallas_call x1, Pallas kernels, body(): pl.pallas_call(functools.partial(kernel, (secs, rows, capacity, chunks)),...  150 us
    unnamed x1, blocking collectives  7.25 us
    unnamed x3, local copies, waits for them, and re-layouts  3.53 us

profile of v1, /device:TPU:1, one launch (start us, length us, event | category | flops | bytes accessed | tf_op | source)
XLA Modules:
  0.0 165.9 jit_solution(9594403978827444096)
XLA Ops:
  0.0 1.2 dynamic-slice
  1.9 0.9 convert_reduce_fusion.1
  2.8 0.7 iota_compare_fusion.3
  3.5 0.8 add_dynamic-update-slice_fusion
  4.3 7.3 %all-reduce = s32[64]{0:T(128)S(1)} all-reduce(s32[64]{0:T(128)S(1)} %add_dynamic-update-slice_fusion), channel_id=1, replica_groups=mesh['groups'=2,'sec'=4,'row'=2,'rep'=2] {'sec'}, use_global_device_ids=true, to_apply=%add | all-reduce | flops 64 | bytes 512
  11.5 0.1 select_reduce_fusion.1
  11.7 0.6 sub.19.fill_ref
  12.3 0.1 reshape.164
  12.4 0.2 convert_reduce_fusion
  12.6 0.2 select_reduce_fusion
  12.8 0.1 reshape.165
  12.8 0.6 and_select_fusion
  13.5 150.1 %shard_map.64 = bf16[16,128,256]{2,1,0:T(8,128)(2,1)} custom-call(s32[32]{0:T(128)} %sub.19.fill_ref, s32[32]{0:T(128)} %get-tuple-element.8.left_ref, s32[32]{0:T(128)} %get-tuple-element.7.right_ref, bf16[16,256,256]{2,1,0:T(8,128)(2,1)} %psi_ref.1, bf16[2,12,128,256]{3,2,1,0:T(8,128)(2,1)} %lenv_ref.1, bf16[2,12,128,256]{3,2,1,0:T(8,128)(2,1)} %renv_ref.1), custom_call_target="tpu_custom_call" | custom-call | flops 12884901888 | bytes 8388608 | tf_op jit(solution)/shard_map/pallas_call | solution.py:334
  163.6 2.3 %copy.9 = bf16[1,16,128,256]{3,2,1,0:T(8,128)(2,1)} copy(bf16[1,16,128,256]{3,2,1,0:T(8,128)(2,1)} %bitcast.4) | data formatting | bytes 2097152
  (7 shorter events, 0.1 us)

commit v2 on v1

--- a/solution.py
+++ b/solution.py
@@ -19,18 +19,22 @@
 def kernel(
     sizes,
     fill_ref,
-    left_ref,
-    right_ref,
+    meta_ref,
     psi_ref,
     lenv_ref,
     renv_ref,
     out_ref,
+    meta_far,
+    codes,
     stage,
     psi_in,
     lfar,
     rfull,
     acc,
     peer,
+    meta_send,
+    meta_recv,
+    code_sem,
     psi_send,
     psi_recv,
     row_send,
@@ -50,6 +54,7 @@
     step = bonds // chunks
     part = width // (2 * rows)
     half = secs // 2
+    unroll = 4 if capacity % 4 == 0 else capacity
     me = lax.axis_index("sec")
     row = lax.axis_index("row")
     rep = lax.axis_index("rep")
@@ -86,7 +91,7 @@
 
     def fill(d):
         for j in range(capacity):
-            p = fill_ref[d * capacity + j]
+            p = lax.shift_right_arithmetic(fill_ref[d, 0, j], 2) - 1
             block = psi_ref[jnp.maximum(p, 0), bars(mine), :]
             stage[d, j] = jnp.where(p >= 0, block, jnp.zeros_like(block))
 
@@ -99,10 +104,24 @@
             {"sec": d},
         )
 
+    def meta_copy(d, source):
+        return remote(
+            meta_ref.at[d],
+            meta_far.at[source],
+            meta_send.at[d],
+            meta_recv.at[source],
+            {"sec": d},
+        )
+
+    def code_copy(source, src):
+        return pltpu.make_async_copy(src.at[source], codes.at[source], code_sem.at[source])
+
     for h in range(1, secs):
         d = lax.rem(me + h, secs)
+        meta_copy(d, me).start()
         fill(d)
         psi_copy(d, me).start()
+    code_copy(me, meta_ref).start()
 
     for c in range(chunks):
 
@@ -114,10 +133,13 @@
         def _():
             l_copy(me, c, chunk_of(c), -1).start()
 
+    def strip(owner):
+        return pl.ds(pl.multiple_of(owner * height, height), height)
+
     def r_copy(h, owner):
         return remote(
             renv_ref,
-            rfull.at[owner],
+            rfull.at[:, :, strip(owner)],
             rrow_send.at[h],
             rrow_recv.at[owner],
             {"row": lax.rem(row + h, rows)},
@@ -125,10 +147,10 @@
 
     for h in range(1, rows):
         r_copy(h, row).start()
-    rfull[row] = renv_ref[...]
+    rfull[:, :, strip(row)] = renv_ref[...]
 
     for j in range(capacity):
-        p = fill_ref[me * capacity + j]
+        p = lax.shift_right_arithmetic(fill_ref[me, 0, j], 2) - 1
         for q in range(2 * rows):
             block = psi_ref[jnp.maximum(p, 0), pl.ds(q * part, part), :]
             psi_in[me, q, j] = jnp.where(p >= 0, block, jnp.zeros_like(block))
@@ -154,6 +176,8 @@
 
     for h in range(1, secs):
         source = lax.rem(me + secs - h, secs)
+        meta_copy(source, source).wait_recv()
+        code_copy(source, meta_far).start()
         psi_copy(source, source).wait_recv()
         for k in range(1, rows):
             row_copy(source, k, lax.rem(row + k, rows)).start()
@@ -177,34 +201,26 @@
             ).wait_recv()
             rep_copy(source, owner).start()
 
-    for h in range(1, secs):
-        source = lax.rem(me + secs - h, secs)
-        for r in range(rows):
-            rep_copy(source, r).wait_recv()
-
     def work(source, c, block):
         def one(j, carry):
-            at = source * capacity + j
-            ls = left_ref[at]
-            rs = right_ref[at]
-            low, high = block(0), block(1)
-            a = jnp.where(ls == 0, low, high).reshape(step * height, width)
+            code = codes[source, 0, j]
+            ls = lax.rem(lax.shift_right_arithmetic(code, 1), 2)
+            rs = lax.rem(code, 2)
+            a = jnp.where(ls == 0, block(0), block(1)).reshape(step * height, width)
             x = psi_in[source, :, j].reshape(width, width)
             product = jnp.dot(a, x, preferred_element_type=jnp.float32).astype(jnp.bfloat16)
-            total = None
-            for w in range(step):
-                b = rfull[:, rs, c * step + w].reshape(width, width)
-                term = jnp.dot(
-                    product[w * height : (w + 1) * height], b, preferred_element_type=jnp.float32
-                )
-                total = term if total is None else total + term
+            wide = jnp.concatenate(
+                [product[w * height : (w + 1) * height] for w in range(step)], axis=1
+            )
+            b = rfull[rs, pl.ds(c * step, step)].reshape(step * width, width)
+            total = jnp.dot(wide, b, preferred_element_type=jnp.float32)
             if c == 0:
                 acc[source, j] = total
             else:
                 acc[source, j] += total
             return carry
 
-        lax.fori_loop(0, capacity, one, 0)
+        lax.fori_loop(0, capacity, one, 0, unroll=unroll)
 
     def sum_copy(source):
         return remote(
@@ -220,9 +236,16 @@
         def _():
             sum_copy(source).start()
 
+    for h in range(secs):
+        code_copy(lax.rem(me + h, secs), meta_ref).wait()
     for c in range(chunks):
         work(me, c, lambda s: lenv_ref[s, pl.ds(c * step, step)])
     hand_over(me)
+
+    for h in range(1, secs):
+        source = lax.rem(me + secs - h, secs)
+        for r in range(rows):
+            rep_copy(source, r).wait_recv()
 
     for h in range(1, secs):
         for c in range(chunks):
@@ -273,6 +296,7 @@
 
     for h in range(1, secs):
         d = lax.rem(me + h, secs)
+        meta_copy(d, me).wait_send()
         psi_copy(d, me).wait_send()
         for k in range(1, rows):
             row_copy(d, k, lax.rem(row + k, rows)).wait_send()
@@ -300,33 +324,21 @@
 
 def body(rows, psi, left_environment_blocks, right_env, pair_dest, pair_left_sector, pair_right):
     secs = lax.axis_size("sec")
-    me = lax.axis_index("sec")
     pairs = psi.shape[0]
     capacity = 2 * pairs // secs
     sectors, bonds, height, width = left_environment_blocks.shape
     chunks = 4
     step = bonds // chunks
     part = width // (2 * rows)
-    code = pair_dest[:, 0] * 4 + pair_left_sector * 2 + pair_right
-    codes = lax.all_gather(code, "sec", axis=0, tiled=True).reshape(secs, pairs)
+    targets = pair_dest[:, 0]
     places = jnp.arange(pairs)
-    slots = jnp.arange(capacity)
-
-    def ranks(dest):
-        same = dest[..., :, None] == dest[..., None, :]
-        earlier = places[None, :] < places[:, None]
-        return jnp.sum((same & earlier).astype(jnp.int32), axis=-1)
-
-    targets = pair_dest[:, 0]
-    match = (targets[None, None, :] == jnp.arange(secs)[:, None, None]) & (
-        ranks(targets)[None, None, :] == slots[None, :, None]
-    )
-    fill = (jnp.sum(match.astype(jnp.int32) * (places + 1), axis=-1) - 1).reshape(-1)
-    dest = codes // 4
-    found = ((dest == me)[:, None, :] & (ranks(dest)[:, None, :] == slots[None, :, None])).astype(
-        jnp.int32
-    )
-    at = jnp.sum(found * (codes % 4)[:, None, :], axis=-1).reshape(-1)
+    same = targets[:, None] == targets[None, :]
+    rank = jnp.sum((same & (places[None, :] < places[:, None])).astype(jnp.int32), axis=-1)
+    value = (places + 1) * 4 + pair_left_sector * 2 + pair_right
+    match = (targets[None, :] == jnp.arange(secs)[:, None])[:, None, :] & (
+        rank[None, :] == jnp.arange(128)[:, None]
+    )[None]
+    meta = jnp.sum(jnp.where(match, value, 0), axis=-1)[:, None, :]
     bf16, f32 = jnp.bfloat16, jnp.float32
     dma = pltpu.SemaphoreType.DMA
     vmem = pl.BlockSpec(memory_space=pltpu.VMEM)
@@ -334,15 +346,20 @@
     out = pl.pallas_call(
         functools.partial(kernel, (secs, rows, capacity, chunks)),
         out_shape=jax.ShapeDtypeStruct((capacity * secs // 2, height, width), bf16),
-        in_specs=[smem, smem, smem, vmem, vmem, vmem],
+        in_specs=[smem, vmem, vmem, vmem, vmem],
         out_specs=vmem,
         scratch_shapes=[
+            pltpu.VMEM((secs, 1, 128), jnp.int32),
+            pltpu.SMEM((secs, 1, 128), jnp.int32),
             pltpu.VMEM((secs, capacity, part, width), bf16),
             pltpu.VMEM((secs, 2 * rows, capacity, part, width), bf16),
             pltpu.VMEM((secs, chunks, sectors, step, height, width), bf16),
-            pltpu.VMEM((rows, sectors, bonds, height, width), bf16),
+            pltpu.VMEM((sectors, bonds, rows * height, width), bf16),
             pltpu.VMEM((secs, capacity, height, width), f32),
             pltpu.VMEM((secs // 2, capacity, height, width), f32),
+            dma((secs,)),
+            dma((secs,)),
+            dma((secs,)),
             dma((secs,)),
             dma((secs,)),
             dma((secs, rows)),
@@ -365,7 +382,7 @@
             bytes_accessed=8 * 1024 * 1024,
             transcendentals=0,
         ),
-    )(fill, at // 2, at % 2, psi, left_environment_blocks, right_env)
+    )(meta, meta, psi, left_environment_blocks, right_env)
     return out[None]
 
 

time: 166 us -> 145 us (0.87)
  Pallas kernels: 150 us -> 139 us
  blocking collectives: 7.25 us -> 0 us
  local copies, waits for them, and re-layouts: 4.29 us -> 2.29 us
    pallas_call x1, Pallas kernels: 150 us -> 139 us  [body(): pl.pallas_call(functools.partial(kernel, (secs, rows, capacity, chunks)),...]
    unnamed x1 -> x0, blocking collectives: 7.25 us -> none
    unnamed x3 -> x1, local copies, waits for them, and re-layouts: 3.53 us -> 2.29 us
where the time goes in v2:
time: 145 us
  Pallas kernels  139 us (96%)
  other arithmetic  3 us (2%)
  local copies, waits for them, and re-layouts  2.29 us (2%)
    pallas_call x1, Pallas kernels, body(): pl.pallas_call(functools.partial(kernel, (secs, rows, capacity, chunks)),...  139 us

profile of v2, /device:TPU:1, one launch (start us, length us, event | category | flops | bytes accessed | tf_op | source)
XLA Modules:
  0.0 144.7 jit_solution(7052115964724323780)
XLA Ops:
  0.0 0.9 convert_reduce_fusion
  0.9 0.7 iota_compare_fusion.2
  1.6 0.7 add_add_fusion
  2.3 0.1 iota_compare_fusion
  2.3 0.7 select_reduce_fusion
  3.0 139.4 %shard_map.64 = bf16[16,128,256]{2,1,0:T(8,128)(2,1)} custom-call(s32[4,1,128]{2,1,0:T(1,128)} %bitcast.4, s32[4,1,128]{2,1,0:T(1,128)} %bitcast.5, bf16[16,256,256]{2,1,0:T(8,128)(2,1)} %psi_ref.1, bf16[2,12,128,256]{3,2,1,0:T(8,128)(2,1)} %lenv_ref.1, bf16[2,12,128,256]{3,2,1,0:T(8,128)(2,1)} %renv_ref.1), custom_call_target="tpu_custom_call" | custom-call | flops 12884901888 | bytes 8388608 | tf_op jit(solution)/shard_map/pallas_call | solution.py:346
  142.4 2.3 %copy.8 = bf16[1,16,128,256]{3,2,1,0:T(8,128)(2,1)} copy(bf16[1,16,128,256]{3,2,1,0:T(8,128)(2,1)} %bitcast.3) | data formatting | bytes 2097152

commit v3 on v2

--- a/solution.py
+++ b/solution.py
@@ -32,6 +32,15 @@
     rfull,
     acc,
     peer,
+    rhelp,
+    ready,
+    land,
+    rh_send,
+    rh_recv,
+    rhrow_send,
+    rhrow_recv,
+    out_send,
+    out_recv,
     meta_send,
     meta_recv,
     code_sem,
@@ -60,6 +69,18 @@
     rep = lax.axis_index("rep")
     other = 1 - rep
     mine = row * 2 + rep
+    last = secs - 1
+    is_end = (me == 0) | (me == last)
+    helper = (me == 1) | (me == last - 1)
+    end = lax.div(me - 1, secs - 3) * last
+    opposite = last - end
+    aide = 1 + lax.div(me, last) * (secs - 3)
+
+    def near(a):
+        return (me + a != last) | ((me != 0) & (me != last))
+
+    def far(a):
+        return (me + a == last) & is_end
 
     def bars(q):
         return pl.ds(pl.multiple_of(q * part, part), part)
@@ -89,6 +110,28 @@
     def chunk_of(c):
         return lenv_ref.at[:, pl.ds(c * step, step)]
 
+    def strip(owner):
+        return pl.ds(pl.multiple_of(owner * height, height), height)
+
+    def help_copy(c):
+        return remote(
+            renv_ref.at[:, pl.ds(c * step, step)],
+            rhelp.at[:, pl.ds(c * step, step), strip(row)],
+            rh_send.at[c],
+            rh_recv.at[c],
+            {"sec": aide},
+        )
+
+    def help_row(c, h, owner):
+        block = rhelp.at[:, pl.ds(c * step, step), strip(owner)]
+        return remote(
+            block,
+            block,
+            rhrow_send.at[c, h],
+            rhrow_recv.at[c, owner],
+            {"row": lax.rem(row + h, rows)},
+        )
+
     def fill(d):
         for j in range(capacity):
             p = lax.shift_right_arithmetic(fill_ref[d, 0, j], 2) - 1
@@ -118,9 +161,27 @@
 
     for h in range(1, secs):
         d = lax.rem(me + h, secs)
-        meta_copy(d, me).start()
         fill(d)
-        psi_copy(d, me).start()
+
+        @pl.when(near(d))
+        def _():
+            meta_copy(d, me).start()
+            psi_copy(d, me).start()
+
+        @pl.when(far(d))
+        def _():
+            to = 1 + lax.div(d, last) * (secs - 3)
+            remote(
+                meta_ref.at[d], meta_far.at[secs], meta_send.at[d], meta_recv.at[secs], {"sec": to}
+            ).start()
+            remote(
+                stage.at[d],
+                psi_in.at[secs, mine],
+                psi_send.at[d],
+                psi_recv.at[secs],
+                {"sec": to},
+            ).start()
+
     code_copy(me, meta_ref).start()
 
     for c in range(chunks):
@@ -133,8 +194,9 @@
         def _():
             l_copy(me, c, chunk_of(c), -1).start()
 
-    def strip(owner):
-        return pl.ds(pl.multiple_of(owner * height, height), height)
+        @pl.when(is_end)
+        def _():
+            help_copy(c).start()
 
     def r_copy(h, owner):
         return remote(
@@ -174,34 +236,55 @@
             {"rep": other},
         )
 
-    for h in range(1, secs):
-        source = lax.rem(me + secs - h, secs)
-        meta_copy(source, source).wait_recv()
-        code_copy(source, meta_far).start()
-        psi_copy(source, source).wait_recv()
+    def arrived(source, at):
+        meta_copy(me, at).wait_recv()
+        code_copy(at, meta_far).start()
+        psi_copy(me, at).wait_recv()
         for k in range(1, rows):
-            row_copy(source, k, lax.rem(row + k, rows)).start()
-        rep_copy(source, row).start()
-
-    for h in range(1, rows):
-        owner = lax.rem(row + h, rows)
-        r_copy(h, owner).wait_recv()
-
-    for h in range(1, secs):
-        source = lax.rem(me + secs - h, secs)
+            row_copy(at, k, lax.rem(row + k, rows)).start()
+        rep_copy(at, row).start()
+
+    def spread(at):
         for k in range(1, rows):
             owner = lax.rem(row + k, rows)
             bar = owner * 2 + rep
             remote(
-                psi_in.at[source, bar],
-                psi_in.at[source, bar],
-                row_send.at[source, k],
-                row_recv.at[source, owner],
+                psi_in.at[at, bar],
+                psi_in.at[at, bar],
+                row_send.at[at, k],
+                row_recv.at[at, owner],
                 {"row": owner},
             ).wait_recv()
-            rep_copy(source, owner).start()
-
-    def work(source, c, block):
+            rep_copy(at, owner).start()
+
+    def spread_done(at):
+        for r in range(rows):
+            rep_copy(at, r).wait_recv()
+
+    def spread_left(at):
+        for k in range(1, rows):
+            row_copy(at, k, lax.rem(row + k, rows)).wait_send()
+        for r in range(rows):
+            rep_copy(at, r).wait_send()
+
+    def each(action):
+        for h in range(1, secs):
+            source = lax.rem(me + secs - h, secs)
+
+            @pl.when(near(source))
+            def _():
+                action(source)
+
+        @pl.when(helper)
+        def _():
+            action(secs)
+
+    each(lambda at: arrived(at, at))
+    for h in range(1, rows):
+        r_copy(h, lax.rem(row + h, rows)).wait_recv()
+    each(spread)
+
+    def work(source, c, block, right):
         def one(j, carry):
             code = codes[source, 0, j]
             ls = lax.rem(lax.shift_right_arithmetic(code, 1), 2)
@@ -212,7 +295,7 @@
             wide = jnp.concatenate(
                 [product[w * height : (w + 1) * height] for w in range(step)], axis=1
             )
-            b = rfull[rs, pl.ds(c * step, step)].reshape(step * width, width)
+            b = right[rs, pl.ds(c * step, step)].reshape(step * width, width)
             total = jnp.dot(wide, b, preferred_element_type=jnp.float32)
             if c == 0:
                 acc[source, j] = total
@@ -231,31 +314,44 @@
             {"rep": other},
         )
 
+    def help_sum():
+        return remote(
+            acc.at[secs], peer.at[half], sum_send.at[secs], sum_recv.at[half], {"rep": other}
+        )
+
+    def out_copy():
+        return remote(ready, land, out_send, out_recv, {"sec": end})
+
+    def forward_help(c):
+        @pl.when(helper)
+        def _():
+            help_copy(c).wait_recv()
+            for h in range(1, rows):
+                help_row(c, h, row).start()
+
     def hand_over(source):
         @pl.when(source // half != rep)
         def _():
             sum_copy(source).start()
 
-    for h in range(secs):
-        code_copy(lax.rem(me + h, secs), meta_ref).wait()
+    code_copy(me, meta_ref).wait()
+    each(lambda at: code_copy(at, meta_far).wait())
     for c in range(chunks):
-        work(me, c, lambda s: lenv_ref[s, pl.ds(c * step, step)])
+        work(me, c, lambda s: lenv_ref[s, pl.ds(c * step, step)], rfull)
     hand_over(me)
-
-    for h in range(1, secs):
-        source = lax.rem(me + secs - h, secs)
-        for r in range(rows):
-            rep_copy(source, r).wait_recv()
-
-    for h in range(1, secs):
+    each(spread_done)
+
+    for h in range(1, last):
         for c in range(chunks):
+            if h == last - 1:
+                forward_help(c)
 
             @pl.when(me >= h)
             def _():
                 source = me - h
                 l_copy(source, c, lfar.at[source, c], 1).wait_recv()
 
-                @pl.when(me + 1 < secs)
+                @pl.when((me + 1 < secs) & ((me != h) | (me + 1 != last)))
                 def _():
                     l_copy(source, c, lfar.at[source, c], 1).start()
 
@@ -264,33 +360,59 @@
                 source = me + h
                 l_copy(source, c, lfar.at[source, c], -1).wait_recv()
 
-                @pl.when(me > 0)
+                @pl.when((me > 0) & ((me != 1) | (me + h != last)))
                 def _():
                     l_copy(source, c, lfar.at[source, c], -1).start()
 
             @pl.when(me >= h)
             def _():
                 source = me - h
-                work(source, c, lambda s: lfar[source, c, s])
+                work(source, c, lambda s: lfar[source, c, s], rfull)
                 if c == chunks - 1:
                     hand_over(source)
 
             @pl.when(me + h < secs)
             def _():
                 source = me + h
-                work(source, c, lambda s: lfar[source, c, s])
+                work(source, c, lambda s: lfar[source, c, s], rfull)
                 if c == chunks - 1:
                     hand_over(source)
 
+    @pl.when(helper)
+    def _():
+        for c in range(chunks):
+            for h in range(1, rows):
+                help_row(c, h, lax.rem(row + h, rows)).wait_recv()
+        for c in range(chunks):
+            work(secs, c, lambda s: lfar[opposite, c, s], rhelp)
+
+        @pl.when(lax.div(opposite, half) != rep)
+        def _():
+            help_sum().start()
+
+        @pl.when(lax.div(opposite, half) == rep)
+        def _():
+            help_sum().wait_recv()
+            for j in range(capacity):
+                ready[j] = (acc[secs, j] + peer[half, j]).astype(ready.dtype)
+            out_copy().start()
+
     def finish(i, carry):
         source = rep * half + i
-        sum_copy(source).wait_recv()
-
-        def one(j, carry):
-            out_ref[i * capacity + j] = (acc[source, j] + peer[i, j]).astype(out_ref.dtype)
-            return carry
-
-        return lax.fori_loop(0, capacity, one, carry)
+
+        @pl.when(near(source))
+        def _():
+            sum_copy(source).wait_recv()
+            for j in range(capacity):
+                out_ref[i * capacity + j] = (acc[source, j] + peer[i, j]).astype(out_ref.dtype)
+
+        @pl.when(far(source))
+        def _():
+            out_copy().wait_recv()
+            for j in range(capacity):
+                out_ref[i * capacity + j] = land[j]
+
+        return carry
 
     lax.fori_loop(0, half, finish, 0)
 
@@ -298,25 +420,45 @@
         d = lax.rem(me + h, secs)
         meta_copy(d, me).wait_send()
         psi_copy(d, me).wait_send()
-        for k in range(1, rows):
-            row_copy(d, k, lax.rem(row + k, rows)).wait_send()
-        for r in range(rows):
-            rep_copy(d, r).wait_send()
+    each(spread_left)
+
+    @pl.when(is_end)
+    def _():
+        for c in range(chunks):
+            help_copy(c).wait_send()
+
+    @pl.when(helper)
+    def _():
+        for c in range(chunks):
+            for h in range(1, rows):
+                help_row(c, h, row).wait_send()
+
+        @pl.when(lax.div(opposite, half) != rep)
+        def _():
+            help_sum().wait_send()
+
+        @pl.when(lax.div(opposite, half) == rep)
+        def _():
+            out_copy().wait_send()
+
     for h in range(1, rows):
         r_copy(h, row).wait_send()
     for c in range(chunks):
         for h in range(secs):
 
-            @pl.when((me >= h) & (me + 1 < secs))
+            @pl.when((me >= h) & (me + 1 < secs) & ((me != h) | (me + 1 != last)))
             def _():
                 l_copy(me - h, c, lfar.at[me - h, c], 1).wait_send()
 
-            @pl.when((me + h < secs) & (me > 0))
+            @pl.when((me + h < secs) & (me > 0) & ((me != 1) | (me + h != last)))
             def _():
                 l_copy(me + h, c, lfar.at[me + h, c], -1).wait_send()
 
     def left(i, carry):
-        sum_copy(other * half + i).wait_send()
+        @pl.when(near(other * half + i))
+        def _():
+            sum_copy(other * half + i).wait_send()
+
         return carry
 
     lax.fori_loop(0, half, left, 0)
@@ -349,30 +491,39 @@
         in_specs=[smem, vmem, vmem, vmem, vmem],
         out_specs=vmem,
         scratch_shapes=[
-            pltpu.VMEM((secs, 1, 128), jnp.int32),
-            pltpu.SMEM((secs, 1, 128), jnp.int32),
+            pltpu.VMEM((secs + 1, 1, 128), jnp.int32),
+            pltpu.SMEM((secs + 1, 1, 128), jnp.int32),
             pltpu.VMEM((secs, capacity, part, width), bf16),
-            pltpu.VMEM((secs, 2 * rows, capacity, part, width), bf16),
+            pltpu.VMEM((secs + 1, 2 * rows, capacity, part, width), bf16),
             pltpu.VMEM((secs, chunks, sectors, step, height, width), bf16),
             pltpu.VMEM((sectors, bonds, rows * height, width), bf16),
-            pltpu.VMEM((secs, capacity, height, width), f32),
-            pltpu.VMEM((secs // 2, capacity, height, width), f32),
+            pltpu.VMEM((secs + 1, capacity, height, width), f32),
+            pltpu.VMEM((secs // 2 + 1, capacity, height, width), f32),
+            pltpu.VMEM((sectors, bonds, rows * height, width), bf16),
+            pltpu.VMEM((capacity, height, width), bf16),
+            pltpu.VMEM((capacity, height, width), bf16),
+            dma((chunks,)),
+            dma((chunks,)),
+            dma((chunks, rows)),
+            dma((chunks, rows)),
+            dma,
+            dma,
             dma((secs,)),
+            dma((secs + 1,)),
+            dma((secs + 1,)),
             dma((secs,)),
-            dma((secs,)),
-            dma((secs,)),
-            dma((secs,)),
-            dma((secs, rows)),
-            dma((secs, rows)),
-            dma((secs, rows)),
-            dma((secs, rows)),
+            dma((secs + 1,)),
+            dma((secs + 1, rows)),
+            dma((secs + 1, rows)),
+            dma((secs + 1, rows)),
+            dma((secs + 1, rows)),
             dma((rows,)),
             dma((rows,)),
             dma((secs, chunks)),
             dma((secs, chunks)),
             dma((secs, chunks)),
-            dma((secs // 2 * 2,)),
-            dma((secs // 2,)),
+            dma((secs + 1,)),
+            dma((secs // 2 + 1,)),
         ],
         compiler_params=pltpu.CompilerParams(
             collective_id=0, has_side_effects=True, vmem_limit_bytes=56 * 1024 * 1024

time: 145 us -> 146 us (level)
  no operation moved by 1% of the time
where the time goes in v3:
time: 146 us
  Pallas kernels  140 us (96%)
  other arithmetic  3 us (2%)
  local copies, waits for them, and re-layouts  2.29 us (2%)
    pallas_call x1, Pallas kernels, body(): pl.pallas_call(functools.partial(kernel, (secs, rows, capacity, chunks)),...  140 us

profile of v3, /device:TPU:1, one launch (start us, length us, event | category | flops | bytes accessed | tf_op | source)
XLA Modules:
  0.0 145.6 jit_solution(11946428165422450117)
XLA Ops:
  0.0 0.9 convert_reduce_fusion
  0.9 0.7 iota_compare_fusion.2
  1.6 0.7 add_add_fusion
  2.3 0.1 iota_compare_fusion
  2.3 0.7 select_reduce_fusion
  3.0 140.3 %shard_map.64 = bf16[16,128,256]{2,1,0:T(8,128)(2,1)} custom-call(s32[4,1,128]{2,1,0:T(1,128)} %bitcast.4, s32[4,1,128]{2,1,0:T(1,128)} %bitcast.5, bf16[16,256,256]{2,1,0:T(8,128)(2,1)} %psi_ref.1, bf16[2,12,128,256]{3,2,1,0:T(8,128)(2,1)} %lenv_ref.1, bf16[2,12,128,256]{3,2,1,0:T(8,128)(2,1)} %renv_ref.1), custom_call_target="tpu_custom_call" | custom-call | flops 12884901888 | bytes 8388608 | tf_op jit(solution)/shard_map/pallas_call | solution.py:488
  143.3 2.3 %copy.8 = bf16[1,16,128,256]{3,2,1,0:T(8,128)(2,1)} copy(bf16[1,16,128,256]{3,2,1,0:T(8,128)(2,1)} %bitcast.3) | data formatting | bytes 2097152

commit v4 on v3

--- a/solution.py
+++ b/solution.py
@@ -295,7 +295,7 @@
             wide = jnp.concatenate(
                 [product[w * height : (w + 1) * height] for w in range(step)], axis=1
             )
-            b = right[rs, pl.ds(c * step, step)].reshape(step * width, width)
+            b = right(rs).reshape(step * width, width)
             total = jnp.dot(wide, b, preferred_element_type=jnp.float32)
             if c == 0:
                 acc[source, j] = total
@@ -329,6 +329,16 @@
             for h in range(1, rows):
                 help_row(c, h, row).start()
 
+    def help_work(c):
+        for h in range(1, rows):
+            help_row(c, h, lax.rem(row + h, rows)).wait_recv()
+
+        def chosen(i):
+            low, high = (rhelp[n, pl.ds(c * step, step)] for n in range(2))
+            return jnp.where(i == 0, low, high)
+
+        work(secs, c, lambda s: lfar[opposite, c, s], chosen)
+
     def hand_over(source):
         @pl.when(source // half != rep)
         def _():
@@ -337,7 +347,7 @@
     code_copy(me, meta_ref).wait()
     each(lambda at: code_copy(at, meta_far).wait())
     for c in range(chunks):
-        work(me, c, lambda s: lenv_ref[s, pl.ds(c * step, step)], rfull)
+        work(me, c, lambda s: lenv_ref[s, pl.ds(c * step, step)], lambda i: rfull[i, pl.ds(c * step, step)])
     hand_over(me)
     each(spread_done)
 
@@ -367,24 +377,26 @@
             @pl.when(me >= h)
             def _():
                 source = me - h
-                work(source, c, lambda s: lfar[source, c, s], rfull)
+                work(source, c, lambda s: lfar[source, c, s], lambda i: rfull[i, pl.ds(c * step, step)])
                 if c == chunks - 1:
                     hand_over(source)
 
             @pl.when(me + h < secs)
             def _():
                 source = me + h
-                work(source, c, lambda s: lfar[source, c, s], rfull)
+                work(source, c, lambda s: lfar[source, c, s], lambda i: rfull[i, pl.ds(c * step, step)])
                 if c == chunks - 1:
                     hand_over(source)
 
+            if h == last - 1 and c > 0:
+
+                @pl.when(helper)
+                def _():
+                    help_work(c - 1)
+
     @pl.when(helper)
     def _():
-        for c in range(chunks):
-            for h in range(1, rows):
-                help_row(c, h, lax.rem(row + h, rows)).wait_recv()
-        for c in range(chunks):
-            work(secs, c, lambda s: lfar[opposite, c, s], rhelp)
+        help_work(chunks - 1)
 
         @pl.when(lax.div(opposite, half) != rep)
         def _():

time: 146 us -> 142 us (0.973)
  Pallas kernels: 140 us -> 136 us
    pallas_call x1, Pallas kernels: 140 us -> 136 us  [body(): pl.pallas_call(functools.partial(kernel, (secs, rows, capacity, chunks)),...]
where the time goes in v4:
time: 142 us
  Pallas kernels  136 us (96%)
  other arithmetic  3 us (2%)
  local copies, waits for them, and re-layouts  2.29 us (2%)
    pallas_call x1, Pallas kernels, body(): pl.pallas_call(functools.partial(kernel, (secs, rows, capacity, chunks)),...  136 us

profile of v4, /device:TPU:1, one launch (start us, length us, event | category | flops | bytes accessed | tf_op | source)
XLA Modules:
  0.0 141.5 jit_solution(12762676803299505240)
XLA Ops:
  0.0 0.9 convert_reduce_fusion
  0.9 0.7 iota_compare_fusion.2
  1.6 0.7 add_add_fusion
  2.3 0.1 iota_compare_fusion
  2.3 0.7 select_reduce_fusion
  3.0 136.2 %shard_map.64 = bf16[16,128,256]{2,1,0:T(8,128)(2,1)} custom-call(s32[4,1,128]{2,1,0:T(1,128)} %bitcast.4, s32[4,1,128]{2,1,0:T(1,128)} %bitcast.5, bf16[16,256,256]{2,1,0:T(8,128)(2,1)} %psi_ref.1, bf16[2,12,128,256]{3,2,1,0:T(8,128)(2,1)} %lenv_ref.1, bf16[2,12,128,256]{3,2,1,0:T(8,128)(2,1)} %renv_ref.1), custom_call_target="tpu_custom_call" | custom-call | flops 12884901888 | bytes 8388608 | tf_op jit(solution)/shard_map/pallas_call | solution.py:500
  139.2 2.3 %copy.8 = bf16[1,16,128,256]{3,2,1,0:T(8,128)(2,1)} copy(bf16[1,16,128,256]{3,2,1,0:T(8,128)(2,1)} %bitcast.3) | data formatting | bytes 2097152
